TPU v7x, 32 devices: a whole 2x2x4 slice. The times are simulated.
32 devices in a mesh: wide: 16 (over z, y, core), narrow: 2 (over x).
Axes of the slice: x: 2, y: 2, z: 4, core: 2. Of those that a mesh axis runs over, the one named last changes fastest.
Arguments:
- right_side: float32 [96, 128, 256], P(('wide', 'narrow')), may hold values from -6 to 6
- diag_inverse: float32 [96, 128, 128], P(('wide', 'narrow')), may hold values from -1 to 1, as said below
- off_tiles: float32 [96, 48, 128, 128], P('wide', 'narrow'), may hold values from -0.078125 to 0.078125
- tile_columns: int32 [96, 48], P('wide', 'narrow'), may hold values from 0 to 95, as said below
- colors: int32 [96], replicated, may hold values from 0 to 2, as said below
Outputs:
- potentials: float32 [96, 128, 256], P(('wide', 'narrow'))
Inputs may be any that keep to these rules, and one draw needn't show every extreme that they name: `colors`: each device along wide+narrow owns 3 consecutive blocks, exactly 1 of each color. `tile_columns`: slot k of a block row names a block owned by a device whose narrow index is k // 24, and of another color than the row's block. `diag_inverse`: symmetric tiles.
All inputs are finite; a program needn't handle non-finite values.
Results may differ from a plain program's by a relative error of at most 0.0001.
Values sent between devices are 32-bit elements; how exact they have to be, the bound alone decides.
A program may use at most 128 MiB of HBM per device.

v0:
```python
from functools import partial

import jax
import jax.numpy as jnp
from jax import lax
from jax.sharding import PartitionSpec as P


def block_terms(stack, tile_rows, column_slots, column_hues, start, count):
    picked = stack[column_hues, column_slots]
    return jnp.einsum("rkab,rkbl->ral", tile_rows, picked, precision=lax.Precision.HIGHEST)


def sweep(source, sorted_inv, sorted_tiles, slot_of, color_of, wide_size, narrow_size, per_color):
    label_width = source.shape[2]
    tile_size = source.shape[1]
    copies = jnp.zeros((3, wide_size * per_color, tile_size, label_width), jnp.float32)
    pieces = [None, None, None]
    for section, color_now in enumerate((0, 1, 2, 1, 0)):
        offset = color_now * per_color
        local_side = source[offset : offset + per_color]
        if section > 0:
            row_low = color_now * narrow_size * per_color
            row_high = row_low + narrow_size * per_color
            term_fn = partial(
                block_terms,
                copies,
                sorted_tiles[row_low:row_high],
                slot_of[row_low:row_high],
                color_of[row_low:row_high],
            )
            summed = lax.psum_scatter(
                term_fn(jnp.int32(0), lax.axis_size("narrow") * per_color),
                "narrow",
                scatter_dimension=0,
                tiled=True,
            )
            local_side = local_side - summed
        updated = jnp.einsum(
            "rab,rbl->ral",
            sorted_inv[offset : offset + per_color],
            local_side,
            precision=lax.Precision.HIGHEST,
        )
        pieces[color_now] = updated
        if section < 4:
            gathered = lax.all_gather(updated, "wide", axis=0, tiled=True)
            copies = copies.at[color_now].set(gathered)
    return jnp.concatenate(pieces, axis=0)


def shards(right_side, diag_inverse, off_tiles, tile_columns, colors):
    wide_size = lax.axis_size("wide")
    narrow_size = lax.axis_size("narrow")
    wide_at = lax.axis_index("wide")
    narrow_at = lax.axis_index("narrow")
    row_count = off_tiles.shape[0]
    own_count = right_side.shape[0]
    per_color = own_count // 3
    block_total = colors.shape[0]
    row_colors = lax.dynamic_slice_in_dim(colors, wide_at * row_count, row_count)
    row_order = jnp.argsort(row_colors, stable=True)
    sorted_tiles = off_tiles[row_order]
    sorted_cols = tile_columns[row_order]
    owner_colors = colors.reshape(block_total // own_count, own_count)
    owner_order = jnp.argsort(owner_colors, axis=1, stable=True)
    owner_inverse = jnp.argsort(owner_order, axis=1)
    ranks = (owner_inverse - owner_colors * per_color).reshape(block_total)
    block_ids = jnp.arange(block_total, dtype=jnp.int32)
    slot_all = block_ids // (narrow_size * own_count) * per_color + ranks
    slot_of = slot_all[sorted_cols]
    color_of = colors[sorted_cols]
    own_start = (wide_at * narrow_size + narrow_at) * own_count
    own_colors = lax.dynamic_slice_in_dim(colors, own_start, own_count)
    own_order = jnp.argsort(own_colors, stable=True)
    own_inverse = jnp.argsort(own_order)
    sorted_inv = diag_inverse[own_order]
    sorted_side = right_side[own_order]
    result = sweep(
        sorted_side, sorted_inv, sorted_tiles, slot_of, color_of, wide_size, narrow_size, per_color
    )
    return result[own_inverse]


def solution(mesh):
    return jax.shard_map(
        shards,
        mesh=mesh,
        in_specs=(
            P(("wide", "narrow"), None, None),
            P(("wide", "narrow"), None, None),
            P("wide", "narrow", None, None),
            P("wide", "narrow"),
            P(),
        ),
        out_specs=P(("wide", "narrow"), None, None),
        check_vma=False,
    )
```

profile of v0, /device:TPU:0, one launch (start us, length us, event | category | flops | bytes accessed | tf_op | source)
XLA Modules:
  0.0 317.8 jit_solution(14142655278700782819)
XLA Ops:
  8.7 1.5 gather_fusion
  10.2 0.9 fusion.8
  12.7 1.0 sort.86
  13.7 1.2 gather_fusion.3
  16.6 1.9 gather_fusion.4
  18.6 1.6 gather_fusion.5
  20.5 8.6 %gather_fusion.2 = f32[6,24,128,128]{3,2,1,0:T(8,128)} fusion(f32[6,24,128,128]{3,2,1,0:T(8,128)} %param.15, s32[1024]{0:T(1024)S(1)} %pad_clamp_fusion.2), kind=kCustom, calls=%fused_computation.2 | custom fusion | bytes 18874392 | tf_op jit(solution)/shard_map/gather | solution.py:63
  29.1 26.3 %all-gather.9.cloned.1.call-done = f32[2048,256]{1,0:T(8,128)} async-done(((f32[128,256]{1,0:T(8,128)}), f32[2048,256]{1,0:T(8,128)}) %all-gather.9.cloned.1.call-update) | async-done | bytes 2097168 | tf_op jit(solution)/shard_map/all_gather | solution.py:47
  55.4 5.1 %scatter.14 = f32[3,16,128,256]{3,2,1,0:T(8,128)} pad(f32[1,16,128,256]{3,2,1,0:T(8,128)} %bitcast.69, f32[]{:T(128)} %constant.133.clone.1), padding=0_2x0_0x0_0x0_0 | pad | bytes 8388612 | tf_op jit(solution)/shard_map/scatter | solution.py:48
  60.4 6.5 %gather_fusion.6 = f32[48,128,256]{2,1,0:T(8,128)} fusion(f32[3,16,128,256]{3,2,1,0:T(8,128)} %scatter.14, s32[48]{0:T(128)S(1)} %reshape.253), kind=kCustom, calls=%fused_computation.6 | custom fusion | bytes 12583296 | tf_op jit(solution)/shard_map/gather | solution.py:10
  66.9 9.7 %convolution_bitcast_fusion.3 = f32[2,128,256]{2,1,0:T(8,128)} fusion(f32[6,24,128,128]{3,2,1,0:T(8,128)} %gather_fusion.2, f32[2,24,128,256]{3,2,1,0:T(8,128)} %bitcast.65), kind=kOutput, calls=%fused_computation.14 | convolution fusion | flops 2415919104 | bytes 15990784 | tf_op jit(solution)/shard_map/rkab,rkbl->ral/dot_general | solution.py:11
  76.7 10.5 %reduce-scatter.5.cloned.1.call-done = f32[1,128,256]{2,1,0:T(8,128)} async-done(((f32[2,128,256]{2,1,0:T(8,128)}), f32[1,128,256]{2,1,0:T(8,128)}) %reduce-scatter.5.cloned.1.call-update) | async-done | bytes 131088 | tf_op jit(solution)/shard_map/reduce_scatter | solution.py:32
  87.3 1.8 fusion.6
  89.4 41.7 %all-gather.11.cloned.1.call-done = f32[2048,256]{1,0:T(8,128)} async-done(((f32[128,256]{1,0:T(8,128)}), f32[2048,256]{1,0:T(8,128)}) %all-gather.11.cloned.1.call-update) | async-done | bytes 2097168 | tf_op jit(solution)/shard_map/all_gather | solution.py:47
  131.1 3.2 %constant_dynamic-update-slice_fusion.2 = f32[3,16,128,256]{3,2,1,0:T(8,128)} fusion(f32[3,16,128,256]{3,2,1,0:T(8,128)} %scatter.14, f32[1,16,128,256]{3,2,1,0:T(8,128)} %bitcast.67), kind=kLoop, calls=%fused_computation.72 | loop fusion | bytes 4194304 | tf_op jit(solution)/shard_map/scatter | solution.py:48
  134.3 6.5 %gather_fusion.7 = f32[48,128,256]{2,1,0:T(8,128)} fusion(f32[3,16,128,256]{3,2,1,0:T(8,128)} %constant_dynamic-update-slice_fusion.2, s32[48]{0:T(128)S(1)} %reshape.259), kind=kCustom, calls=%fused_computation.7 | custom fusion | bytes 12583296 | tf_op jit(solution)/shard_map/gather | solution.py:10
  140.8 9.7 %convolution_bitcast_fusion.2 = f32[2,128,256]{2,1,0:T(8,128)} fusion(f32[6,24,128,128]{3,2,1,0:T(8,128)} %gather_fusion.2, f32[2,24,128,256]{3,2,1,0:T(8,128)} %bitcast.63), kind=kOutput, calls=%fused_computation.13 | convolution fusion | flops 2415919104 | bytes 15990784 | tf_op jit(solution)/shard_map/rkab,rkbl->ral/dot_general | solution.py:11
  150.6 10.5 %reduce-scatter.7.cloned.1.call-done = f32[1,128,256]{2,1,0:T(8,128)} async-done(((f32[2,128,256]{2,1,0:T(8,128)}), f32[1,128,256]{2,1,0:T(8,128)}) %reduce-scatter.7.cloned.1.call-update) | async-done | bytes 131088 | tf_op jit(solution)/shard_map/reduce_scatter | solution.py:32
  161.2 1.8 fusion.1
  163.2 41.4 %all-gather.13.cloned.1.call-done = f32[2048,256]{1,0:T(8,128)} async-done(((f32[128,256]{1,0:T(8,128)}), f32[2048,256]{1,0:T(8,128)}) %all-gather.13.cloned.1.call-update) | async-done | bytes 2097168 | tf_op jit(solution)/shard_map/all_gather | solution.py:47
  204.6 3.1 constant_dynamic-update-slice_fusion.1
  207.7 6.5 %gather_fusion.8 = f32[48,128,256]{2,1,0:T(8,128)} fusion(f32[3,16,128,256]{3,2,1,0:T(8,128)} %constant_dynamic-update-slice_fusion.1, s32[48]{0:T(128)S(1)} %reshape.253), kind=kCustom, calls=%fused_computation.8 | custom fusion | bytes 12583296 | tf_op jit(solution)/shard_map/gather | solution.py:10
  214.2 9.7 %convolution_bitcast_fusion.1 = f32[2,128,256]{2,1,0:T(8,128)} fusion(f32[6,24,128,128]{3,2,1,0:T(8,128)} %gather_fusion.2, f32[2,24,128,256]{3,2,1,0:T(8,128)} %bitcast.64), kind=kOutput, calls=%fused_computation.12 | convolution fusion | flops 2415919104 | bytes 15990784 | tf_op jit(solution)/shard_map/rkab,rkbl->ral/dot_general | solution.py:11
  224.0 10.5 %reduce-scatter.9.cloned.1.call-done = f32[1,128,256]{2,1,0:T(8,128)} async-done(((f32[2,128,256]{2,1,0:T(8,128)}), f32[1,128,256]{2,1,0:T(8,128)}) %reduce-scatter.9.cloned.1.call-update) | async-done | bytes 131088 | tf_op jit(solution)/shard_map/reduce_scatter | solution.py:32
  234.5 1.8 fusion.4
  236.7 41.7 %all-gather.15.cloned.1.call-done = f32[2048,256]{1,0:T(8,128)} async-done(((f32[128,256]{1,0:T(8,128)}), f32[2048,256]{1,0:T(8,128)}) %all-gather.15.cloned.1.call-update) | async-done | bytes 2097168 | tf_op jit(solution)/shard_map/all_gather | solution.py:47
  278.4 3.2 %constant_dynamic-update-slice_fusion = f32[3,16,128,256]{3,2,1,0:T(8,128)} fusion(f32[3,16,128,256]{3,2,1,0:T(8,128)} %constant_dynamic-update-slice_fusion.1, f32[1,16,128,256]{3,2,1,0:T(8,128)} %bitcast.66), kind=kLoop, calls=%fused_computation.70 | loop fusion | bytes 4194304 | tf_op jit(solution)/shard_map/scatter | solution.py:48
  281.6 6.5 %gather_fusion.9 = f32[48,128,256]{2,1,0:T(8,128)} fusion(f32[3,16,128,256]{3,2,1,0:T(8,128)} %constant_dynamic-update-slice_fusion, s32[48]{0:T(128)S(1)} %reshape.271), kind=kCustom, calls=%fused_computation.9 | custom fusion | bytes 12583296 | tf_op jit(solution)/shard_map/gather | solution.py:10
  288.1 9.8 %convolution_bitcast_fusion = f32[2,128,256]{2,1,0:T(8,128)} fusion(f32[6,24,128,128]{3,2,1,0:T(8,128)} %gather_fusion.2, f32[2,24,128,256]{3,2,1,0:T(8,128)} %bitcast.62), kind=kOutput, calls=%fused_computation.11 | convolution fusion | flops 2415919104 | bytes 15990784 | tf_op jit(solution)/shard_map/rkab,rkbl->ral/dot_general | solution.py:11
  298.6 9.8 %reduce-scatter.11.cloned.1.call-done = f32[1,128,256]{2,1,0:T(8,128)} async-done(((f32[2,128,256]{2,1,0:T(8,128)}), f32[1,128,256]{2,1,0:T(8,128)}) %reduce-scatter.11.cloned.1.call-update) | async-done | bytes 131088 | tf_op jit(solution)/shard_map/reduce_scatter | solution.py:32
  308.5 1.2 convolution_bitcast_fusion.4
  309.7 1.3 gather_fusion.10
  (64 shorter events, 7.6 us)
Async XLA Ops:
  6.5 1.6 copy-start
  6.5 48.8 %all-gather.9.cloned.1.call-start = ((), (), s32[]{:S(2)}) async-start(), calls=%async_computation.8 | async-start | bytes 2228224 | tf_op jit(solution)/shard_map/all_gather | solution.py:47
  11.1 76.2 %reduce-scatter.5.cloned.1.call-start = ((), (), s32[]{:S(2)}) async-start(), calls=%async_computation.4 | async-start | bytes 393216 | tf_op jit(solution)/shard_map/reduce_scatter | solution.py:32
  76.7 54.4 %all-gather.11.cloned.1.call-start = ((), (), s32[]{:S(2)}) async-start(), calls=%async_computation.9 | async-start | bytes 2228224 | tf_op jit(solution)/shard_map/all_gather | solution.py:47
  89.1 72.1 %reduce-scatter.7.cloned.1.call-start = ((), (), s32[]{:S(2)}) async-start(), calls=%async_computation.5 | async-start | bytes 393216 | tf_op jit(solution)/shard_map/reduce_scatter | solution.py:32
  150.6 54.0 %all-gather.13.cloned.1.call-start = ((), (), s32[]{:S(2)}) async-start(), calls=%async_computation.10 | async-start | bytes 2228224 | tf_op jit(solution)/shard_map/all_gather | solution.py:47
  163.0 71.5 %reduce-scatter.9.cloned.1.call-start = ((), (), s32[]{:S(2)}) async-start(), calls=%async_computation.6 | async-start | bytes 393216 | tf_op jit(solution)/shard_map/reduce_scatter | solution.py:32
  223.9 54.4 %all-gather.15.cloned.1.call-start = ((), (), s32[]{:S(2)}) async-start(), calls=%async_computation.11 | async-start | bytes 2228224 | tf_op jit(solution)/shard_map/all_gather | solution.py:47
  236.4 72.1 %reduce-scatter.11.cloned.1.call-start = ((), (), s32[]{:S(2)}) async-start(), calls=%async_computation.7 | async-start | bytes 393216 | tf_op jit(solution)/shard_map/reduce_scatter | solution.py:32
  288.1 21.6 %copy-start.1 = (f32[128,256]{1,0:T(8,128)S(1)}, f32[128,256]{1,0:T(8,128)}, u32[]{:S(2)}) copy-start(f32[128,256]{1,0:T(8,128)} %fusion.1) | copy-start | bytes 393220
  288.1 21.6 %copy-start.2 = (f32[128,256]{1,0:T(8,128)S(1)}, f32[128,256]{1,0:T(8,128)}, u32[]{:S(2)}) copy-start(f32[128,256]{1,0:T(8,128)} %fusion.4) | copy-start | bytes 393220
Sparse Core Ops, SparseCore 0:
  11.2 44.0 all-gather.8
  76.8 10.4 reduce-scatter.4
  89.7 41.4 all-gather.10
  150.7 10.4 reduce-scatter.6
  163.2 41.3 all-gather.12
  224.1 10.4 reduce-scatter.8
  236.9 41.4 all-gather.14
  298.0 10.4 reduce-scatter.10
where the time goes:
time: 318 us
  waiting for transfers between devices  193 us (61%)
  local copies, waits for them, and re-layouts  60.7 us (19%)
  matrix products  46.6 us (15%)
  between operations  13.6 us (4%)
  other arithmetic  3.94 us (1%)
    all_gather x4, waiting for transfers between devices, sweep(): gathered = lax.all_gather(updated, 'wide', axis=0, tiled=True)  151 us
    reduce_scatter x4, waiting for transfers between devices, sweep(): lax.psum_scatter(term_fn(jnp.int32(0), lax.axis_size('narrow') * per_colo...  41.4 us
    dot_general x4, matrix products, block_terms(): jnp.einsum('rkab,rkbl->ral', tile_rows, picked, precision=lax.Precision.H...  39 us
    gather x4, local copies, waits for them, and re-layouts, block_terms(): picked = stack[column_hues, column_slots]  26 us
    scatter x4, local copies, waits for them, and re-layouts, sweep(): copies = copies.at[color_now].set(gathered)  14.5 us
    gather x1, local copies, waits for them, and re-layouts, shards(): sorted_tiles = off_tiles[row_order]  8.58 us
    dot_general x5, matrix products, sweep(): jnp.einsum('rab,rbl->ral', sorted_inv[offset:offset + per_color], local_s...  7.55 us
  transfers between devices with their start and end apart: 8, of which 8 were waited for; matrix products, arithmetic and copies ran while one was open for 6% of the time, Pallas kernels for 0%

commit v1 on v0

v1 whole, which is shorter than its diff:
```python
import functools

import jax
import jax.numpy as jnp
from jax import lax
from jax.experimental import pallas as pl
from jax.experimental.pallas import tpu as pltpu
from jax.sharding import PartitionSpec as P

MESH = pl.DeviceIdType.MESH
HALF = 128


def split(value):
    high = value.astype(jnp.bfloat16)
    low = (value - high.astype(jnp.float32)).astype(jnp.bfloat16)
    return high, low


def fold(wide_sum):
    t = wide_sum.shape[0] // 2
    return (wide_sum[:t, :HALF] + wide_sum[:t, HALF:]) + (wide_sum[t:, :HALF] + wide_sum[t:, HALF:])


def kernel(
    n_wide, n_narrow, colors, columns, side_ref, diag_ref, tiles_ref, out_ref,
    stage, ta, da, vb, gathered, psend, precv, xout, index, acc, own_sum,
    load_sem, ring_send, ring_recv, sib_send, sib_recv, part_send, part_recv,
):
    wide = lax.axis_index("wide")
    narrow = lax.axis_index("narrow")
    rows, kd = stage.shape[0], stage.shape[1]
    pairs = kd // 2
    chips = n_wide // 2
    depth = chips // 2
    zs = chips // 2
    chip, core = lax.div(wide, 2), lax.rem(wide, 2)
    z, y = lax.div(chip, 2), lax.rem(chip, 2)
    here = z + y * (2 * zs - 1 - 2 * z)

    def at(position, which):
        q = lax.rem(position + 2 * chips, chips)
        qy = lax.div(q, zs)
        qz = q + qy * (2 * zs - 1 - 2 * q)
        return (qz * 2 + qy) * 2 + which

    right, left, sibling = at(here + 1, core), at(here - 1, core), at(here, 1 - core)

    for r in range(rows):
        pltpu.make_async_copy(tiles_ref.at[r], stage.at[r], load_sem.at[r]).start()

    for h in range(2):
        @pl.loop(0, 3 * n_wide)
        def _(i):
            vb[h, i] = jnp.zeros(vb.shape[2:], jnp.bfloat16)

    def pick(color, owner_narrow):
        base = (wide * n_narrow + owner_narrow) * 3
        return jnp.where(colors[base + 1] == color, 1, jnp.where(colors[base + 2] == color, 2, 0))

    barrier = pltpu.get_barrier_semaphore()
    for peer in (right, left, sibling):
        pl.semaphore_signal(barrier, inc=1, device_id=(peer, narrow), device_id_type=MESH)
    for d in range(1, n_narrow):
        peer = lax.rem(narrow + d, n_narrow)
        pl.semaphore_signal(barrier, inc=1, device_id=(wide, peer), device_id_type=MESH)
    pl.semaphore_wait(barrier, 3 + n_narrow - 1)

    def ring_copy(s, h, origin, rel, target):
        ref = gathered.at[s, h, origin]
        return pltpu.make_async_remote_copy(
            src_ref=ref, dst_ref=ref, send_sem=ring_send.at[s, h, rel], recv_sem=ring_recv.at[s, h, rel],
            device_id=(target, narrow), device_id_type=MESH,
        )

    def sib_copy(s, h, origin, rel):
        ref = gathered.at[s, h, origin]
        return pltpu.make_async_remote_copy(
            src_ref=ref, dst_ref=ref, send_sem=sib_send.at[s, h, rel], recv_sem=sib_recv.at[s, h, rel],
            device_id=(sibling, narrow), device_id_type=MESH,
        )

    def part_copy(s, h, d):
        target = lax.rem(narrow + d, n_narrow)
        return pltpu.make_async_remote_copy(
            src_ref=psend.at[s, h, d - 1], dst_ref=precv.at[s, h, d - 1],
            send_sem=part_send.at[s, h, d - 1], recv_sem=part_recv.at[s, h, d - 1],
            device_id=(wide, target), device_id_type=MESH,
        )

    def color_of(s):
        return s - 2 * jnp.maximum(s - 2, 0)

    def keep(s, h, origin):
        high, low = split(gathered[s, h, origin])
        spot = color_of(s) * n_wide + origin
        vb[h, spot, :, 0:HALF] = high
        vb[h, spot, :, HALF:] = low

    def reach(h):
        return (depth, depth - 1) if h == 0 else (depth - 1, depth)

    def start_gather(s, h):
        ring_copy(s, h, wide, 1, right).start()
        ring_copy(s, h, wide, chips - 1, left).start()
        sib_copy(s, h, wide, 0).start()
        keep(s, h, wide)

    def arrivals(h, j):
        if j == 0:
            return [0]
        r, l = reach(h)
        return ([j] if j <= r else []) + ([chips - j] if j <= l else [])

    def take_sibling(s, h, j):
        for rel in arrivals(h, j):
            origin = at(here - rel, 1 - core)
            sib_copy(s, h, origin, rel).wait_recv()
            keep(s, h, origin)

    def relay(s, h, j):
        r, l = reach(h)
        for rel in arrivals(h, j):
            origin = at(here - rel, core)
            rightward = rel == j and j <= r
            ring_copy(s, h, origin, rel, right if rightward else left).wait_recv()
            if rightward and j < r:
                ring_copy(s, h, origin, rel + 1, right).start()
            if not rightward and j < l:
                ring_copy(s, h, origin, rel - 1, left).start()
            sib_copy(s, h, origin, rel).start()
        for rel in arrivals(h, j):
            keep(s, h, at(here - rel, core))
        take_sibling(s, h, j - 1)

    def solve(s, h, side):
        color = color_of(s)
        high, low = split(side)
        rhs = jnp.concatenate([high, low], axis=1)
        return fold(jnp.dot(da[color], rhs, preferred_element_type=jnp.float32))

    def columns_of(h):
        return slice(h * HALF, (h + 1) * HALF)

    for color in range(3):
        high, low = split(diag_ref[pick(color, narrow)])
        t = high.shape[0]
        da[color, 0:t] = high
        da[color, t:] = low

    for h in range(2):
        gathered[0, h, wide] = solve(0, h, side_ref[pick(0, narrow), :, columns_of(h)])
        start_gather(0, h)

    for color in range(3):
        @pl.loop(0, n_narrow)
        def _(n):
            row = n * 3 + pick(color, n)

            @pl.loop(0, kd)
            def _(k):
                column = columns[row, k]
                index[(color * n_narrow + n) * kd + k] = colors[column] * n_wide + lax.div(column, 3 * n_narrow)

    for r in range(rows):
        pltpu.make_async_copy(tiles_ref.at[r], stage.at[r], load_sem.at[r]).wait()

    done = 0
    for turn, color in enumerate((1, 2, 0)):
        @pl.loop(0, n_narrow)
        def _(n):
            row = n * 3 + pick(color, n)
            t = stage.shape[2]

            @pl.loop(0, kd // 2)
            def _(k):
                for part in range(2):
                    high, low = split(stage[row, 2 * k + part])
                    ta[color * n_narrow + n, k, 0:t, part * t:(part + 1) * t] = high
                    ta[color * n_narrow + n, k, t:, part * t:(part + 1) * t] = low

        while done < depth * (turn + 1) // 3:
            done += 1
            relay(0, 0, done)
            if done > 1:
                relay(0, 1, done - 1)

    cuts = max(1, min(pairs, depth // n_narrow))
    pieces = cuts * n_narrow

    def section(s, h, step, first, last):
        color = color_of(s)
        take_sibling(s - 1, h, depth)
        count, at_step = 0, first
        for d in list(range(1, n_narrow)) + [0]:
            target = lax.rem(narrow + d, n_narrow)
            group = color * n_narrow + target
            for cut in range(cuts):
                total = None
                for k in range(cut * pairs // cuts, (cut + 1) * pairs // cuts):
                    spot = group * kd + 2 * k
                    rhs = jnp.concatenate([vb[h, index[spot]], vb[h, index[spot + 1]]], axis=0)
                    term = jnp.dot(ta[group, k], rhs, preferred_element_type=jnp.float32)
                    total = term if total is None else total + term
                if cut == 0:
                    acc[...] = fold(total)
                else:
                    acc[...] += fold(total)
                if cut == cuts - 1:
                    if d > 0:
                        psend[s - 1, h, d - 1] = acc[...]
                        part_copy(s - 1, h, d).start()
                    else:
                        own_sum[...] = acc[...]
                count += 1
                while at_step <= last and (at_step - first) < (last - first + 1) * count // pieces:
                    step(at_step)
                    at_step += 1
        summed = own_sum[...]
        for d in range(1, n_narrow):
            part_copy(s - 1, h, d).wait_recv()
            summed = summed + precv[s - 1, h, d - 1]
        x = solve(s, h, side_ref[pick(color, narrow), :, columns_of(h)] - summed)
        xout[color, :, columns_of(h)] = x

        @pl.when(s < 4)
        def _():
            gathered[s, h, wide] = x
            start_gather(s, h)

    def both(s, carry):
        def step_one(j):
            relay(s - 1, 1, j)

        def step_zero(j):
            @pl.when(s < 4)
            def _():
                relay(s, 0, j)

        @pl.when(s == 1)
        def _():
            relay(0, 1, depth)

        @pl.when(s > 1)
        def _():
            relay(s - 1, 1, 1)

        section_zero(s, step_one)
        section(s, 1, step_zero, 1, depth)
        return carry

    def section_zero(s, step_one):
        def guarded(j):
            @pl.when(s > 1)
            def _():
                step_one(j)

        section(s, 0, guarded, 2, depth)

    lax.fori_loop(1, 5, both, 0)

    for j in range(3):
        out_ref[j] = xout[colors[(wide * n_narrow + narrow) * 3 + j]]

    @pl.loop(0, 4)
    def _(s):
        for h in range(2):
            @pl.loop(0, chips)
            def _(rel):
                sib_copy(s, h, wide, rel).wait_send()

            @pl.loop(1, chips)
            def _(rel):
                ring_copy(s, h, wide, rel, right).wait_send()

            for d in range(1, n_narrow):
                part_copy(s, h, d).wait_send()


def shards(n_wide, n_narrow, right_side, diag_inverse, off_tiles, tile_columns, colors):
    own, tile, labels = right_side.shape
    rows, kd = off_tiles.shape[:2]
    chips = n_wide // 2
    others = n_narrow - 1
    f32, b16 = jnp.float32, jnp.bfloat16
    dma = pltpu.SemaphoreType.DMA
    vmem = pl.BlockSpec(memory_space=pltpu.VMEM)
    smem = pl.BlockSpec(memory_space=pltpu.SMEM)
    return pl.pallas_call(
        functools.partial(kernel, n_wide, n_narrow),
        out_shape=jax.ShapeDtypeStruct((own, tile, labels), f32),
        in_specs=[smem, smem, vmem, vmem, pl.BlockSpec(memory_space=pl.ANY)],
        out_specs=vmem,
        scratch_shapes=[
            pltpu.VMEM((rows, kd, tile, tile), f32),
            pltpu.VMEM((rows, kd // 2, 2 * tile, 2 * tile), b16),
            pltpu.VMEM((3, 2 * tile, tile), b16),
            pltpu.VMEM((2, 3 * n_wide, tile, 2 * HALF), b16),
            pltpu.VMEM((4, 2, n_wide, tile, HALF), f32),
            pltpu.VMEM((4, 2, others, tile, HALF), f32),
            pltpu.VMEM((4, 2, others, tile, HALF), f32),
            pltpu.VMEM((3, tile, labels), f32),
            pltpu.SMEM((rows * kd,), jnp.int32),
            pltpu.VMEM((tile, HALF), f32),
            pltpu.VMEM((tile, HALF), f32),
            dma((rows,)),
            dma((4, 2, chips)),
            dma((4, 2, chips)),
            dma((4, 2, chips)),
            dma((4, 2, chips)),
            dma((4, 2, others)),
            dma((4, 2, others)),
        ],
        compiler_params=pltpu.CompilerParams(
            collective_id=0, has_side_effects=True, vmem_limit_bytes=63 * 1024 * 1024
        ),
        cost_estimate=pl.CostEstimate(flops=8 * 10**9, bytes_accessed=10**7, transcendentals=0),
    )(colors, tile_columns, right_side, diag_inverse, off_tiles)


def solution(mesh):
    return jax.shard_map(
        functools.partial(shards, mesh.shape["wide"], mesh.shape["narrow"]),
        mesh=mesh,
        in_specs=(
            P(("wide", "narrow"), None, None),
            P(("wide", "narrow"), None, None),
            P("wide", "narrow", None, None),
            P("wide", "narrow"),
            P(),
        ),
        out_specs=P(("wide", "narrow"), None, None),
        check_vma=False,
    )
```

time: 318 us -> 123 us (0.39)
  waiting for transfers between devices: 193 us -> 0 us
  Pallas kernels: 0 us -> 121 us
  local copies, waits for them, and re-layouts: 60.7 us -> 1.77 us
  matrix products: 46.6 us -> 0 us
  between operations: 13.6 us -> 0.01 us
  other arithmetic: 3.94 us -> 0 us
    all_gather x4 -> x0, waiting for transfers between devices: 151 us -> none  [sweep(): gathered = lax.all_gather(updated, 'wide', axis=0, tiled=True)]
    pallas_call x0 -> x1, Pallas kernels: none -> 121 us  [shards(): pl.pallas_call(functools.partial(kernel, n_wide, n_narrow), out_shape=jax...]
    dot_general x9 -> x0, matrix products: 46.6 us -> none  [the longest x4 39 us: block_terms(): jnp.einsum('rkab,rkbl->ral', tile_rows, picked, precision=lax.Precision.H...]
    gather x11 -> x0, local copies, waits for them, and re-layouts: 42.6 us -> none  [the longest x4 26 us: block_terms(): picked = stack[column_hues, column_slots]]
    reduce_scatter x4 -> x0, waiting for transfers between devices: 41.4 us -> none  [sweep(): lax.psum_scatter(term_fn(jnp.int32(0), lax.axis_size('narrow') * per_colo...]
    scatter x4 -> x0, local copies, waits for them, and re-layouts: 14.5 us -> none  [sweep(): copies = copies.at[color_now].set(gathered)]
    sort x5 -> x0, other arithmetic: 3.82 us -> none  [the longest x1 1.04 us: shards(): row_order = jnp.argsort(row_colors, stable=True)]
  transfers between devices with their start and end apart: 8 -> 0, of which waited for: 8 -> 0; matrix products, arithmetic and copies ran while one was open for 6% -> 0% of each run, Pallas kernels for 0% -> 0%
where the time goes in v1:
time: 123 us
  Pallas kernels  121 us (98%)
  local copies, waits for them, and re-layouts  1.77 us (1%)
    pallas_call x1, Pallas kernels, shards(): pl.pallas_call(functools.partial(kernel, n_wide, n_narrow), out_shape=jax...  121 us

profile of v1, /device:TPU:0, one launch (start us, length us, event | category | flops | bytes accessed | tf_op | source)
XLA Modules:
  0.0 123.0 jit_solution(5671984438352443025)
XLA Ops:
  0.0 121.2 %shard_map.55 = f32[3,128,256]{2,1,0:T(8,128)} custom-call(s32[96]{0:T(128)} %colors.1, s32[6,24]{1,0:T(8,128)} %columns.1, f32[3,128,256]{2,1,0:T(8,128)} %side_ref.1, f32[3,128,128]{2,1,0:T(8,128)} %diag_ref.1, f32[6,24,128,128]{3,2,1,0:T(8,128)} %tiles_ref.1), custom_call_target="tpu_custom_call" | custom-call | flops 8000000000 | bytes 10000000 | tf_op jit(solution)/shard_map/pallas_call | solution.py:289
  121.2 1.8 %copy.7 = f32[3,128,256]{2,1,0:T(8,128)} copy(f32[3,128,256]{2,1,0:T(8,128)} %shard_map.55) | data formatting | bytes 786432

commit v2 on v1

--- a/solution.py
+++ b/solution.py
@@ -32,19 +32,15 @@
     rows, kd = stage.shape[0], stage.shape[1]
     pairs = kd // 2
     chips = n_wide // 2
-    depth = chips // 2
     zs = chips // 2
     chip, core = lax.div(wide, 2), lax.rem(wide, 2)
     z, y = lax.div(chip, 2), lax.rem(chip, 2)
-    here = z + y * (2 * zs - 1 - 2 * z)
-
-    def at(position, which):
-        q = lax.rem(position + 2 * chips, chips)
-        qy = lax.div(q, zs)
-        qz = q + qy * (2 * zs - 1 - 2 * q)
-        return (qz * 2 + qy) * 2 + which
-
-    right, left, sibling = at(here + 1, core), at(here - 1, core), at(here, 1 - core)
+
+    def at(at_z, at_y, which):
+        return (lax.rem(at_z + zs, zs) * 2 + at_y) * 2 + which
+
+    across, sibling = at(z, 1 - y, core), at(z, y, 1 - core)
+    steps = sorted(range(1, zs), key=lambda d: min(d, zs - d))
 
     for r in range(rows):
         pltpu.make_async_copy(tiles_ref.at[r], stage.at[r], load_sem.at[r]).start()
@@ -59,12 +55,12 @@
         return jnp.where(colors[base + 1] == color, 1, jnp.where(colors[base + 2] == color, 2, 0))
 
     barrier = pltpu.get_barrier_semaphore()
-    for peer in (right, left, sibling):
+    for peer in [across, sibling] + [at(z + d, y, core) for d in steps]:
         pl.semaphore_signal(barrier, inc=1, device_id=(peer, narrow), device_id_type=MESH)
     for d in range(1, n_narrow):
         peer = lax.rem(narrow + d, n_narrow)
         pl.semaphore_signal(barrier, inc=1, device_id=(wide, peer), device_id_type=MESH)
-    pl.semaphore_wait(barrier, 3 + n_narrow - 1)
+    pl.semaphore_wait(barrier, 1 + zs + n_narrow - 1)
 
     def ring_copy(s, h, origin, rel, target):
         ref = gathered.at[s, h, origin]
@@ -97,41 +93,33 @@
         vb[h, spot, :, 0:HALF] = high
         vb[h, spot, :, HALF:] = low
 
-    def reach(h):
-        return (depth, depth - 1) if h == 0 else (depth - 1, depth)
-
     def start_gather(s, h):
-        ring_copy(s, h, wide, 1, right).start()
-        ring_copy(s, h, wide, chips - 1, left).start()
+        ring_copy(s, h, wide, zs, across).start()
+        for d in steps:
+            ring_copy(s, h, wide, d, at(z + d, y, core)).start()
         sib_copy(s, h, wide, 0).start()
         keep(s, h, wide)
 
-    def arrivals(h, j):
-        if j == 0:
-            return [0]
-        r, l = reach(h)
-        return ([j] if j <= r else []) + ([chips - j] if j <= l else [])
-
-    def take_sibling(s, h, j):
-        for rel in arrivals(h, j):
-            origin = at(here - rel, 1 - core)
-            sib_copy(s, h, origin, rel).wait_recv()
+    def middle(s, h):
+        for d in steps:
+            origin = at(z - d, y, core)
+            ring_copy(s, h, origin, d, across).wait_recv()
+            ring_copy(s, h, origin, zs + d, across).start()
+            sib_copy(s, h, origin, d).start()
+        for d in steps:
+            keep(s, h, at(z - d, y, core))
+
+    def finish(s, h):
+        for d in [0] + steps:
+            origin = at(z - d, 1 - y, core)
+            ring_copy(s, h, origin, zs + d, across).wait_recv()
+            sib_copy(s, h, origin, zs + d).start()
             keep(s, h, origin)
-
-    def relay(s, h, j):
-        r, l = reach(h)
-        for rel in arrivals(h, j):
-            origin = at(here - rel, core)
-            rightward = rel == j and j <= r
-            ring_copy(s, h, origin, rel, right if rightward else left).wait_recv()
-            if rightward and j < r:
-                ring_copy(s, h, origin, rel + 1, right).start()
-            if not rightward and j < l:
-                ring_copy(s, h, origin, rel - 1, left).start()
-            sib_copy(s, h, origin, rel).start()
-        for rel in arrivals(h, j):
-            keep(s, h, at(here - rel, core))
-        take_sibling(s, h, j - 1)
+        for column in range(2):
+            for d in [0] + steps:
+                origin = at(z - d, y + column * (1 - 2 * y), 1 - core)
+                sib_copy(s, h, origin, column * zs + d).wait_recv()
+                keep(s, h, origin)
 
     def solve(s, h, side):
         color = color_of(s)
@@ -165,7 +153,6 @@
     for r in range(rows):
         pltpu.make_async_copy(tiles_ref.at[r], stage.at[r], load_sem.at[r]).wait()
 
-    done = 0
     for turn, color in enumerate((1, 2, 0)):
         @pl.loop(0, n_narrow)
         def _(n):
@@ -179,19 +166,14 @@
                     ta[color * n_narrow + n, k, 0:t, part * t:(part + 1) * t] = high
                     ta[color * n_narrow + n, k, t:, part * t:(part + 1) * t] = low
 
-        while done < depth * (turn + 1) // 3:
-            done += 1
-            relay(0, 0, done)
-            if done > 1:
-                relay(0, 1, done - 1)
-
-    cuts = max(1, min(pairs, depth // n_narrow))
-    pieces = cuts * n_narrow
-
-    def section(s, h, step, first, last):
+        if turn < 2:
+            middle(0, turn)
+
+    cuts = 2 if pairs % 2 == 0 else 1
+
+    def section(s, h, step):
         color = color_of(s)
-        take_sibling(s - 1, h, depth)
-        count, at_step = 0, first
+        finish(s - 1, h)
         for d in list(range(1, n_narrow)) + [0]:
             target = lax.rem(narrow + d, n_narrow)
             group = color * n_narrow + target
@@ -212,10 +194,7 @@
                         part_copy(s - 1, h, d).start()
                     else:
                         own_sum[...] = acc[...]
-                count += 1
-                while at_step <= last and (at_step - first) < (last - first + 1) * count // pieces:
-                    step(at_step)
-                    at_step += 1
+        step()
         summed = own_sum[...]
         for d in range(1, n_narrow):
             part_copy(s - 1, h, d).wait_recv()
@@ -229,33 +208,19 @@
             start_gather(s, h)
 
     def both(s, carry):
-        def step_one(j):
-            relay(s - 1, 1, j)
-
-        def step_zero(j):
+        def move_one():
+            @pl.when(s > 1)
+            def _():
+                middle(s - 1, 1)
+
+        def move_zero():
             @pl.when(s < 4)
             def _():
-                relay(s, 0, j)
-
-        @pl.when(s == 1)
-        def _():
-            relay(0, 1, depth)
-
-        @pl.when(s > 1)
-        def _():
-            relay(s - 1, 1, 1)
-
-        section_zero(s, step_one)
-        section(s, 1, step_zero, 1, depth)
+                middle(s, 0)
+
+        section(s, 0, move_one)
+        section(s, 1, move_zero)
         return carry
-
-    def section_zero(s, step_one):
-        def guarded(j):
-            @pl.when(s > 1)
-            def _():
-                step_one(j)
-
-        section(s, 0, guarded, 2, depth)
 
     lax.fori_loop(1, 5, both, 0)
 
@@ -271,7 +236,7 @@
 
             @pl.loop(1, chips)
             def _(rel):
-                ring_copy(s, h, wide, rel, right).wait_send()
+                ring_copy(s, h, wide, rel, across).wait_send()
 
             for d in range(1, n_narrow):
                 part_copy(s, h, d).wait_send()

time: 123 us -> 90.5 us (0.74)
  Pallas kernels: 121 us -> 88.6 us
    pallas_call x1, Pallas kernels: 121 us -> 88.6 us  [shards(): pl.pallas_call(functools.partial(kernel, n_wide, n_narrow), out_shape=jax...]
where the time goes in v2:
time: 90.5 us; the launch traced here: 90.3 us
  Pallas kernels  88.6 us (98%)
  local copies, waits for them, and re-layouts  1.77 us (2%)
    pallas_call x1, Pallas kernels, shards(): pl.pallas_call(functools.partial(kernel, n_wide, n_narrow), out_shape=jax...  88.6 us

profile of v2, /device:TPU:0, one launch (start us, length us, event | category | flops | bytes accessed | tf_op | source)
XLA Modules:
  0.0 90.3 jit_solution(10427774366233250428)
XLA Ops:
  0.0 88.6 %shard_map.55 = f32[3,128,256]{2,1,0:T(8,128)} custom-call(s32[96]{0:T(128)} %colors.1, s32[6,24]{1,0:T(8,128)} %columns.1, f32[3,128,256]{2,1,0:T(8,128)} %side_ref.1, f32[3,128,128]{2,1,0:T(8,128)} %diag_ref.1, f32[6,24,128,128]{3,2,1,0:T(8,128)} %tiles_ref.1), custom_call_target="tpu_custom_call" | custom-call | flops 8000000000 | bytes 10000000 | tf_op jit(solution)/shard_map/pallas_call | solution.py:254
  88.6 1.8 %copy.7 = f32[3,128,256]{2,1,0:T(8,128)} copy(f32[3,128,256]{2,1,0:T(8,128)} %shard_map.55) | data formatting | bytes 786432

commit v3 on v2

--- a/solution.py
+++ b/solution.py
@@ -192,9 +192,10 @@
                     if d > 0:
                         psend[s - 1, h, d - 1] = acc[...]
                         part_copy(s - 1, h, d).start()
+                        if d == n_narrow - 1:
+                            step()
                     else:
                         own_sum[...] = acc[...]
-        step()
         summed = own_sum[...]
         for d in range(1, n_narrow):
             part_copy(s - 1, h, d).wait_recv()

time: 90.5 us -> 89.2 us (0.986)
  Pallas kernels: 88.6 us -> 87.3 us
    pallas_call x1, Pallas kernels: 88.6 us -> 87.3 us  [shards(): pl.pallas_call(functools.partial(kernel, n_wide, n_narrow), out_shape=jax...]
where the time goes in v3:
time: 89.2 us; the launch traced here: 89 us
  Pallas kernels  87.3 us (98%)
  local copies, waits for them, and re-layouts  1.77 us (2%)
    pallas_call x1, Pallas kernels, shards(): pl.pallas_call(functools.partial(kernel, n_wide, n_narrow), out_shape=jax...  87.3 us

profile of v3, /device:TPU:0, one launch (start us, length us, event | category | flops | bytes accessed | tf_op | source)
XLA Modules:
  0.0 89.0 jit_solution(11486360274862928902)
XLA Ops:
  0.0 87.3 %shard_map.55 = f32[3,128,256]{2,1,0:T(8,128)} custom-call(s32[96]{0:T(128)} %colors.1, s32[6,24]{1,0:T(8,128)} %columns.1, f32[3,128,256]{2,1,0:T(8,128)} %side_ref.1, f32[3,128,128]{2,1,0:T(8,128)} %diag_ref.1, f32[6,24,128,128]{3,2,1,0:T(8,128)} %tiles_ref.1), custom_call_target="tpu_custom_call" | custom-call | flops 8000000000 | bytes 10000000 | tf_op jit(solution)/shard_map/pallas_call | solution.py:255
  87.3 1.8 %copy.7 = f32[3,128,256]{2,1,0:T(8,128)} copy(f32[3,128,256]{2,1,0:T(8,128)} %shard_map.55) | data formatting | bytes 786432
